TPU v7x, 32 devices: a whole 2x2x4 slice. The times are simulated.
32 devices in a mesh: row: 8 (over z, y), col: 4 (over x, core).
Axes of the slice: x: 2, y: 2, z: 4, core: 2. Of those that a mesh axis runs over, the one named last changes fastest.
Arguments:
- density_values: float32 [2048, 512], P('row', 'col'), may hold values from -5 to 5
- density_cols: int32 [32, 8], P('row', 'col'), may hold values from 0 to 31, as said below
- ks_cols: int32 [32, 16], P('row', 'col'), may hold values from 0 to 31, as said below
- core_hamiltonian: float32 [2048, 1024], P('row', 'col'), may hold values from -3 to 3
- tile_blocks: int32 [64, 16], P('row'), may hold values from 0 to 31, as said below
- grid_weights: float32 [64, 128], P('row'), may hold values from 0.5 to 2
- basis_values: float32 [64, 128, 1024], P('row'), may hold values from -1.5 to 1.5
Outputs:
- kohn_sham: float32 [2048, 1024], P('row', 'col')
- purified: float32 [2048, 512], P('row', 'col')
Inputs may be any that keep to these rules, and one draw needn't show every extreme that they name: `density_cols`: for each block row and each index c of col, the 2 entries in slots c * 2 .. c * 2 + 1 are different block columns of c * 8 .. c * 8 + 7. `ks_cols`: for each block row and each index c of col, the 4 entries in slots c * 4 .. c * 4 + 3 are different block columns of c * 8 .. c * 8 + 7. `tile_blocks`: each tile names 16 different blocks.
All inputs are finite; a program needn't handle non-finite values.
Results may differ from a plain program's by a relative error of at most 0.0003.
Values sent between devices are 32-bit elements; how exact they have to be, the bound alone decides.
A program may use at most 128 MiB of HBM per device.

v0:
```python
import functools
import jax
import jax.numpy as jnp
from jax import lax
from jax.experimental import pallas as pl
from jax.experimental.pallas import tpu as pltpu
from jax.sharding import PartitionSpec as P

BS = 64
TB = 16
G = 128
PAIR = 2 * BS
VMEM_BUDGET = 52 * 1024 * 1024


def split(x):
    high = x.astype(jnp.bfloat16)
    return high, (x - high.astype(jnp.float32)).astype(jnp.bfloat16)


def dot(a, b):
    return jnp.dot(a, b, preferred_element_type=jnp.float32)


def dot3(ah, al, bh, bl):
    return dot(ah, bh) + (dot(ah, bl) + dot(al, bh))


def lane_half():
    return (lax.broadcasted_iota(jnp.int32, (1, PAIR), 1) >= BS).astype(jnp.float32)


def widen(values, codes, out_h, out_l, row, first_lane, pairs):
    half = lane_half()
    swapped = pltpu.roll(values, BS, 1)
    swapped_codes = pltpu.roll(jnp.broadcast_to(codes, (8, PAIR)), BS, 1)[0:1]
    for p in range(pairs):
        block = 2.0 * p + half
        dense = jnp.where(codes == block, values, 0.0) + jnp.where(
            swapped_codes == block, swapped, 0.0
        )
        high, low = split(dense)
        lanes = pl.ds(first_lane + p * PAIR, PAIR)
        out_h[pl.ds(row, BS), lanes] = high
        out_l[pl.ds(row, BS), lanes] = low


MESH = pl.DeviceIdType.MESH


def mega_kernel(
    places, basis, packed, weights, core,
    kohn, purified,
    bh, bl, sources, by_row, by_col, dh, dl, oh, ol, product, kept, parts_out, parts_in, turned, wh, wl,
    chunk, pair_out, pair_in, mid, line_in,
    row_send, row_recv, pass_send, col_send, col_recv, part_send, part_recv,
    pair_send, pair_recv, line_send, line_recv,
    *, row_blocks, ks_slots, entry_count,
):
    row_count, col_count = by_row.shape[0], by_col.shape[0]
    row, col = lax.axis_index("row"), lax.axis_index("col")
    side, place = row % 2, row // 2
    line = row_count // 2
    partner = 2 * place + 1 - side
    rows = row_blocks * BS
    tiles = basis.shape[0]
    points = tiles * G
    width = dh.shape[1]
    pairs = width // PAIR
    half = lane_half()

    def on_line(d):
        return 2 * lax.rem(place + d, line) + side

    def col_at(d):
        return lax.rem(col + d, col_count)

    def remote(src, dst, send, recv, to_row, to_col):
        return pltpu.make_async_remote_copy(
            src_ref=src, dst_ref=dst, send_sem=send, recv_sem=recv,
            device_id=(to_row, to_col), device_id_type=MESH,
        )

    barrier = pltpu.get_barrier_semaphore()
    pl.semaphore_signal(barrier, inc=1, device_id=(partner, col), device_id_type=MESH)
    for d in range(1, line):
        pl.semaphore_signal(barrier, inc=1, device_id=(on_line(d), col), device_id_type=MESH)
    for d in range(1, col_count):
        pl.semaphore_signal(barrier, inc=1, device_id=(row, col_at(d)), device_id_type=MESH)
    pl.semaphore_wait(barrier, line + col_count - 1)

    own_sends = []
    for d in range(1, line):
        own_sends.append(
            remote(packed, by_row.at[row], row_send.at[d], row_recv.at[row], on_line(d), col)
        )
    own_sends.append(remote(packed, by_row.at[row], row_send.at[0], row_recv.at[row], partner, col))
    for d in range(1, col_count):
        own_sends.append(
            remote(packed, by_col.at[col], col_send.at[d], col_recv.at[col], row, col_at(d))
        )
    for copy in own_sends:
        copy.start()
    by_row[row] = packed[...]
    by_col[col] = packed[...]

    source_pairs = basis.shape[2] // PAIR
    sources[0, source_pairs] = jnp.zeros((G, PAIR), jnp.float32)
    sources[1, source_pairs] = jnp.zeros((G, PAIR), jnp.float32)

    def expand(t):
        for p in range(source_pairs):
            x = basis[t, :, p * PAIR : (p + 1) * PAIR]
            sources[0, p] = x
            sources[1, p] = pltpu.roll(x, BS, 1)
        at = pl.ds(pl.multiple_of(t * G, G), G)
        for d in range(bh.shape[1] // PAIR):
            left = places[t, 2 * d]
            right = places[t, 2 * d + 1]
            dense = jnp.where(
                half == 0.0,
                sources[left % 2, left // 2],
                sources[1 - right % 2, right // 2],
            )
            high, low = split(dense)
            bh[at, d * PAIR : (d + 1) * PAIR] = high
            bl[at, d * PAIR : (d + 1) * PAIR] = low

    pl.loop(0, tiles // 2)(expand)

    passed = []
    for d in range(1, line):
        origin = 2 * lax.rem(place + line - d, line) + side
        remote(
            packed, by_row.at[origin], row_send.at[d], row_recv.at[origin], partner, col
        ).wait_recv()
        copy = remote(
            by_row.at[origin], by_row.at[origin], pass_send.at[d], row_recv.at[origin], partner, col
        )
        copy.start()
        passed.append(copy)

    pl.loop(tiles // 2, tiles)(expand)

    for d in range(1, col_count):
        origin = col_at(d)
        remote(
            packed, by_col.at[origin], col_send.at[d], col_recv.at[origin], row, origin
        ).wait_recv()
    for d in range(line):
        origin = 2 * lax.rem(place + line - d, line) + 1 - side
        remote(
            packed, by_row.at[origin], row_send.at[0], row_recv.at[origin], partner, col
        ).wait_recv()

    def widen_row(r):
        for l in range(row_blocks):
            at = pl.multiple_of((r * row_blocks + l) * BS, BS)
            widen(
                by_row[r, l * BS : (l + 1) * BS, :],
                by_row[r, rows + l : rows + l + 1, :],
                dh, dl, at, 0, pairs,
            )

    pl.loop(0, row_count)(widen_row)
    for c in range(col_count):
        for l in range(row_blocks):
            widen(
                by_col[c, l * BS : (l + 1) * BS, :],
                by_col[c, rows + l : rows + l + 1, :],
                oh, ol, l * BS, c * width, pairs,
            )

    step = 4 * G
    mine = pl.ds(pl.multiple_of(col * width, PAIR), width)

    @pl.loop(0, points // step)
    def _(s):
        at = pl.ds(pl.multiple_of(s * step, step), step)
        x = dot3(bh[at, :], bl[at, :], dh[...], dl[...])
        local = bh[at, mine].astype(jnp.float32) + bl[at, mine].astype(jnp.float32)
        sums = jnp.sum(x * local, axis=1, keepdims=True)
        for t in range(step // G):
            tile = jnp.broadcast_to(sums[t * G : (t + 1) * G], (G, G))
            parts_out[pl.ds(s * (step // G) + t, 1), :] = tile.T[0:1, :]

    product[...] = dot3(oh[...], ol[...], dh[...], dl[...])
    total = jnp.zeros((BS, PAIR), jnp.float32)
    for l in range(row_blocks):
        codes_here = packed[rows + l : rows + l + 1, :]
        block = jnp.zeros((BS, PAIR), jnp.float32)
        for p in range(pairs):
            piece = product[l * BS : (l + 1) * BS, p * PAIR : (p + 1) * PAIR]
            block += jnp.where(codes_here == 2.0 * p + half, piece, 0.0)
            block += jnp.where(
                codes_here == 2.0 * p + 1.0 - half, pltpu.roll(piece, BS, 1), 0.0
            )
        kept[l * BS : (l + 1) * BS, :] = block
        total += block * block
    square = jnp.sum(jnp.sum(total, axis=1, keepdims=True), axis=0, keepdims=True)
    parts_out[tiles : tiles + 8, :] = jnp.broadcast_to(square, (8, PAIR))

    part_sends = []
    for d in range(1, col_count):
        copy = remote(
            parts_out, parts_in.at[col], part_send.at[d], part_recv.at[col], row, col_at(d)
        )
        copy.start()
        part_sends.append(copy)
    parts_in[col] = parts_out[...]
    for t in range(tiles):
        at = pl.ds(t * G, G)
        local = bh[at, mine].astype(jnp.float32) + bl[at, mine].astype(jnp.float32)
        turned[:, t * G : (t + 1) * G] = local.T
    for d in range(1, col_count):
        origin = col_at(d)
        remote(
            parts_out, parts_in.at[origin], part_send.at[d], part_recv.at[origin], row, origin
        ).wait_recv()
    sums = parts_in[0]
    for c in range(1, col_count):
        sums += parts_in[c]
    potential = weights[...] * jnp.tanh(sums[0:tiles, :])
    for t in range(tiles):
        high, low = split(turned[:, t * G : (t + 1) * G] * potential[t : t + 1, :])
        wh[:, t * G : (t + 1) * G] = high
        wl[:, t * G : (t + 1) * G] = low
    lanes = core.shape[0]
    stored = ks_slots * BS
    square_all = jnp.broadcast_to(sums[tiles : tiles + 1, 0:1], (8, lanes))

    def contribute(owner, out, i):
        at = pl.ds(pl.multiple_of(owner * lanes, PAIR), lanes)
        chunk[...] = dot3(wh[...], wl[...], bh[:, at], bl[:, at])
        for h in range(lanes // PAIR):
            here = slice(h * PAIR, (h + 1) * PAIR)
            for s in range(ks_slots):
                line_at = rows + row_blocks + h * ks_slots + s
                code = by_row[owner, line_at : line_at + 1, :]
                block = jnp.zeros((BS, PAIR), jnp.float32)
                for k in range(width // BS):
                    block += jnp.where(code == float(k), chunk[k * BS : (k + 1) * BS, here], 0.0)
                out[i, s * BS : (s + 1) * BS, here] = block
        out[i, stored : stored + 8, :] = square_all

    def pair_copy(i):
        return remote(
            pair_out.at[i], pair_in.at[i], pair_send.at[i], pair_recv.at[i], partner, col
        )

    def line_copy(i):
        return remote(
            mid.at[i], line_in.at[i], line_send.at[i], line_recv.at[i], on_line(i + 1), col
        )

    def join(i):
        pair_copy(i).wait_recv()
        mid[i] = mid[i] + pair_in[i]

    @pl.loop(0, line)
    def _(i):
        owner = on_line(i + 1)
        contribute(owner + 1 - 2 * side, pair_out, i)
        pair_copy(i).start()
        contribute(owner, mid, i)

        @pl.when(i >= 1)
        def _():
            join(i - 1)
            line_copy(i - 1).start()

    join(line - 1)
    result = mid[line - 1]
    for i in range(line - 1):
        line_copy(i).wait_recv()
        result += line_in[i]
    kohn[...] = core[...] + result[0:stored, :].T
    mean_square = result[stored : stored + 1, 0:1] / entry_count
    purified[...] = kept[...] / jnp.sqrt(mean_square + 1e-06)

    for copy in own_sends + passed + part_sends:
        copy.wait_send()
    for i in range(line):
        pair_copy(i).wait_send()
    for i in range(line - 1):
        line_copy(i).wait_send()


def plain(
    density_values, density_cols, ks_cols, core_hamiltonian, tile_blocks, grid_weights, basis_values
):
    highest = lax.Precision.HIGHEST
    row_blocks, own_slots = density_cols.shape
    ks_slots = ks_cols.shape[1]
    panel, panel_cols, panel_ks = (
        lax.all_gather(density_values, "row", axis=0, tiled=True),
        lax.all_gather(density_cols, "row", axis=0, tiled=True),
        lax.all_gather(ks_cols, "row", axis=0, tiled=True),
    )
    all_blocks = panel_cols.shape[0]
    panel_blocks = panel.reshape(all_blocks, BS, own_slots, BS)
    empty = jnp.zeros((row_blocks, BS, own_slots, BS), jnp.float32)
    values = lax.all_gather(density_values, "col", axis=1, tiled=True)
    columns = lax.all_gather(density_cols, "col", axis=1, tiled=True)
    width = columns.shape[1]
    left_blocks = values.reshape(row_blocks, BS, width, BS)
    neighbours = panel_blocks[columns]
    their_cols = panel_cols[columns]
    matches = (their_cols[:, :, :, None] == density_cols[:, None, None, :]).astype(jnp.float32)
    combined = jnp.einsum("ipqr,ipaqh->iprah", matches, neighbours, precision=highest)
    product = empty + jnp.einsum("ifpa,iprah->ifrh", left_blocks, combined, precision=highest)
    kept = product.reshape(row_blocks * BS, own_slots * BS)
    total_square = lax.psum(jnp.sum(kept * kept), ("row", "col"))
    entry_count = all_blocks * BS * own_slots * lax.axis_size("col") * BS
    purified = kept / jnp.sqrt(total_square / entry_count + 1e-06)
    tile_count = tile_blocks.shape[0]
    basis = basis_values.reshape(tile_count, G, TB, BS)
    tile_rows = panel_blocks[tile_blocks]
    tile_cols = panel_cols[tile_blocks]
    halves = jnp.einsum("tgif,tifqh->tgiqh", basis, tile_rows, precision=highest)
    matches = (tile_cols[:, :, :, None] == tile_blocks[:, None, None, :]).astype(jnp.float32)
    combined = jnp.einsum("tiqj,tgiqh->tgjh", matches, halves, precision=highest)
    partial_density = jnp.sum(combined * basis, axis=(2, 3))
    grid_density = lax.psum(partial_density, "col")
    potential = grid_weights * jnp.tanh(grid_density)
    weighted = basis * potential[:, :, None, None]
    ks_here = panel_ks[tile_blocks]
    ks_matches = (ks_here[:, :, :, None] == tile_blocks[:, None, None, :]).astype(jnp.float32)
    selected = jnp.einsum("tisj,tgjh->tgish", ks_matches, basis, precision=highest)
    pairs = jnp.einsum("tgif,tgish->tifsh", weighted, selected, precision=highest)
    ks_panel = jnp.zeros((all_blocks, BS, ks_slots, BS), jnp.float32)
    ks_panel = ks_panel.at[tile_blocks.reshape(-1)].add(
        pairs.reshape(tile_count * TB, BS, ks_slots, BS)
    )
    own_rows = lax.psum_scatter(
        ks_panel.reshape(all_blocks * BS, ks_slots * BS), "row", scatter_dimension=0, tiled=True
    )
    kohn_sham = core_hamiltonian + own_rows
    return (kohn_sham, purified)


def dense(
    density_values, density_cols, ks_cols, core_hamiltonian, tile_blocks, grid_weights, basis_values
):
    row_blocks, own_slots = density_cols.shape
    ks_slots = ks_cols.shape[1]
    row_count, col_count = lax.axis_size("row"), lax.axis_size("col")
    all_blocks = row_blocks * row_count
    col_blocks = all_blocks // col_count
    width = col_blocks * BS
    order = all_blocks * BS
    tiles = tile_blocks.shape[0]
    points = tiles * G
    rows = row_blocks * BS
    line = row_count // 2
    stored = ks_slots * BS
    col = lax.axis_index("col")
    f32, bf16 = jnp.float32, jnp.bfloat16
    vmem, smem = pl.BlockSpec(memory_space=pltpu.VMEM), pl.BlockSpec(memory_space=pltpu.SMEM)

    local_codes = jnp.repeat((density_cols - col * col_blocks).astype(f32), BS, axis=1)
    local_ks = jnp.repeat((ks_cols - col * col_blocks).astype(f32).T, BS, axis=1)
    ks_lines = [local_ks[:, at : at + PAIR] for at in range(0, rows, PAIR)]
    used = rows + row_blocks + ks_slots * (rows // PAIR)
    fill = jnp.zeros((-used % 16, PAIR), f32)
    packed = jnp.concatenate([density_values, local_codes, *ks_lines, fill], axis=0)

    blocks = jnp.arange(all_blocks, dtype=jnp.int32)
    index = jnp.arange(TB, dtype=jnp.int32)
    same = tile_blocks[:, :, None] == blocks[None, None, :]
    places = jnp.min(jnp.where(same, index[None, :, None], TB), axis=1).astype(jnp.int32)

    dma = pltpu.SemaphoreType.DMA
    kernel = functools.partial(
        mega_kernel,
        row_blocks=row_blocks,
        ks_slots=ks_slots,
        entry_count=float(order * own_slots * col_count * BS),
    )
    packed_rows = packed.shape[0]
    return tuple(
        pl.pallas_call(
            kernel,
            out_shape=[
                jax.ShapeDtypeStruct((rows, stored), f32),
                jax.ShapeDtypeStruct((rows, PAIR), f32),
            ],
            in_specs=[smem] + [vmem] * 4,
            out_specs=[vmem, vmem],
            scratch_shapes=[
                pltpu.VMEM((points, order), bf16),
                pltpu.VMEM((points, order), bf16),
                pltpu.VMEM((2, TB // 2 + 1, G, PAIR), f32),
                pltpu.VMEM((row_count, packed_rows, PAIR), f32),
                pltpu.VMEM((col_count, packed_rows, PAIR), f32),
                pltpu.VMEM((order, width), bf16),
                pltpu.VMEM((order, width), bf16),
                pltpu.VMEM((rows, order), bf16),
                pltpu.VMEM((rows, order), bf16),
                pltpu.VMEM((rows, width), f32),
                pltpu.VMEM((rows, PAIR), f32),
                pltpu.VMEM((tiles + 8, PAIR), f32),
                pltpu.VMEM((col_count, tiles + 8, PAIR), f32),
                pltpu.VMEM((width, points), f32),
                pltpu.VMEM((width, points), bf16),
                pltpu.VMEM((width, points), bf16),
                pltpu.VMEM((width, rows), f32),
                pltpu.VMEM((line, stored + 8, rows), f32),
                pltpu.VMEM((line, stored + 8, rows), f32),
                pltpu.VMEM((line, stored + 8, rows), f32),
                pltpu.VMEM((line, stored + 8, rows), f32),
                dma((line,)),
                dma((row_count,)),
                dma((line,)),
                dma((col_count,)),
                dma((col_count,)),
                dma((col_count,)),
                dma((col_count,)),
                dma((line,)),
                dma((line,)),
                dma((line,)),
                dma((line,)),
            ],
            compiler_params=pltpu.CompilerParams(
                vmem_limit_bytes=VMEM_BUDGET, collective_id=0, has_side_effects=True
            ),
            cost_estimate=pl.CostEstimate(
                flops=12 * points * order * width,
                bytes_accessed=4 * points * TB * BS,
                transcendentals=points,
            ),
            name="kohn_sham_build",
        )(places, basis_values, packed, grid_weights, core_hamiltonian)
    )


def on_device(*args):
    density_cols, tile_blocks = args[1], args[4]
    all_blocks = density_cols.shape[0] * lax.axis_size("row")
    order = all_blocks * BS
    width = order // lax.axis_size("col")
    points = tile_blocks.shape[0] * G
    held = 4 * points * order + 4 * order * width + 4 * points * TB * BS
    fits = held + 16 * points * width < VMEM_BUDGET
    regular = density_cols.shape[1] * BS == PAIR and density_cols.shape[0] % 2 == 0
    regular = regular and lax.axis_size("row") % 2 == 0
    if fits and regular and width % PAIR == 0 and tile_blocks.shape[0] % 8 == 0:
        return dense(*args)
    return plain(*args)


def solution(mesh):
    in_specs = (
        P("row", "col"),
        P("row", "col"),
        P("row", "col"),
        P("row", "col"),
        P("row", None),
        P("row", None),
        P("row", None, None),
    )
    out_specs = (P("row", "col"), P("row", "col"))
    return jax.shard_map(
        on_device, mesh=mesh, in_specs=in_specs, out_specs=out_specs, check_vma=False
    )
```

profile of v0, /device:TPU:9, one launch (start us, length us, event | category | flops | bytes accessed | tf_op | source)
XLA Modules:
  0.0 83.6 jit_solution(10380737693671065443)
XLA Ops:
  0.6 0.7 subtract_convert_fusion
  1.3 0.1 copy.11
  1.4 0.7 convert_bitcast_fusion
  2.1 0.1 copy.12
  2.2 0.1 broadcast_in_dim.26
  2.3 0.1 reshape.11
  2.4 0.8 select_reduce_fusion.places
  3.1 0.1 broadcast_in_dim.27
  3.2 0.1 reshape.12
  3.3 1.0 %concatenate.3.packed = f32[272,128]{1,0:T(8,128)S(1)} concatenate(f32[256,128]{1,0:T(8,128)} %param.7, f32[4,128]{1,0:T(4,128)S(1)} %reshape.11, f32[4,128]{1,0:T(4,128)S(1)} %get-tuple-element.3, f32[4,128]{1,0:T(4,128)S(1)} %get-tuple-element.2, f32[4,128]{1,0:T(4,128)S(1)} %broadcast_in_dim.28), dimensions={0} | concatenate | bytes 278528 | tf_op jit(solution)/shard_map/concatenate | solution.py:366
  4.3 0.0 copy-start
  4.3 0.9 %copy-done = f32[256,256]{1,0:T(8,128)S(1)} copy-done((f32[256,256]{1,0:T(8,128)S(1)}, f32[256,256]{1,0:T(8,128)}, u32[]{:S(2)}) %copy-start) | copy-done | bytes 262168
  5.2 0.0 copy-start.1
  5.2 0.7 copy-done.1
  5.9 76.3 %kohn_sham_build.1 = (f32[256,256]{1,0:T(8,128)S(1)}, f32[256,128]{1,0:T(8,128)S(1)}) custom-call(s32[8,32]{1,0:T(8,128)S(1)} %select_reduce_fusion.places, f32[8,128,1024]{2,1,0:T(8,128)} %basis.1, f32[272,128]{1,0:T(8,128)S(1)} %concatenate.3.packed, f32[8,128]{1,0:T(8,128)S(1)} %copy-done.1, f32[256,256]{1,0:T(8,128)S(1)} %copy-done), custom_call_target="tpu_custom_call" | custom-call | flops 12884901888 | bytes 4194304 | tf_op jit(solution)/shard_map/kohn_sham_build/pallas_call | solution.py:382
  82.2 0.7 copy.15
  82.9 0.7 copy.16
  (2 shorter events, 0.0 us)
Async XLA Ops:
  4.3 0.9 %copy-start = (f32[256,256]{1,0:T(8,128)S(1)}, f32[256,256]{1,0:T(8,128)}, u32[]{:S(2)}) copy-start(f32[256,256]{1,0:T(8,128)} %core.1) | copy-start | bytes 786436
  5.2 0.7 copy-start.1
where the time goes:
time: 83.9 us; the launch traced here: 83.6 us
  Pallas kernels  76.3 us (91%)
  local copies, waits for them, and re-layouts  4.46 us (5%)
  other arithmetic  2.15 us (3%)
    pallas_call x1, Pallas kernels, dense(): pl.pallas_call(kernel, out_shape=[jax.ShapeDtypeStruct((rows, stored), f3...  76.3 us
    unnamed x6, local copies, waits for them, and re-layouts  3 us

commit v1 on v0

--- a/solution.py
+++ b/solution.py
@@ -49,12 +49,12 @@
 
 
 def mega_kernel(
-    places, basis, packed, weights, core,
+    places, density_cols, ks_cols, basis_hbm, values, weights, core,
     kohn, purified,
-    bh, bl, sources, by_row, by_col, dh, dl, oh, ol, product, kept, parts_out, parts_in, turned, wh, wl,
+    basis, packed, acc, square_out, square_in, bh, bl, sources, by_row, by_col, dh, dl, oh, ol, product, kept, parts_out, parts_in, turned, wh, wl,
     chunk, pair_out, pair_in, mid, line_in,
     row_send, row_recv, pass_send, col_send, col_recv, part_send, part_recv,
-    pair_send, pair_recv, line_send, line_recv,
+    pair_send, pair_recv, line_send, line_recv, square_send, square_recv, basis_sem,
     *, row_blocks, ks_slots, entry_count,
 ):
     row_count, col_count = by_row.shape[0], by_col.shape[0]
@@ -81,12 +81,30 @@
             device_id=(to_row, to_col), device_id_type=MESH,
         )
 
+    load_basis = pltpu.make_async_copy(basis_hbm, basis, basis_sem)
+    load_basis.start()
     barrier = pltpu.get_barrier_semaphore()
     pl.semaphore_signal(barrier, inc=1, device_id=(partner, col), device_id_type=MESH)
     for d in range(1, line):
         pl.semaphore_signal(barrier, inc=1, device_id=(on_line(d), col), device_id_type=MESH)
     for d in range(1, col_count):
         pl.semaphore_signal(barrier, inc=1, device_id=(row, col_at(d)), device_id_type=MESH)
+    base = col * (width // BS)
+
+    def code_line(left, right):
+        both = jnp.where(half == 0.0, left - base, right - base)
+        return both.astype(jnp.float32)
+
+    packed[0:rows, :] = values[...]
+    for l in range(row_blocks):
+        packed[rows + l : rows + l + 1, :] = code_line(density_cols[l, 0], density_cols[l, 1])
+    used = rows + row_blocks
+    for h in range(row_blocks // 2):
+        for slot in range(ks_slots):
+            packed[used : used + 1, :] = code_line(ks_cols[2 * h, slot], ks_cols[2 * h + 1, slot])
+            used += 1
+    if used < packed.shape[0]:
+        packed[used:, :] = jnp.zeros((packed.shape[0] - used, PAIR), jnp.float32)
     pl.semaphore_wait(barrier, line + col_count - 1)
 
     own_sends = []
@@ -126,7 +144,10 @@
             bh[at, d * PAIR : (d + 1) * PAIR] = high
             bl[at, d * PAIR : (d + 1) * PAIR] = low
 
-    pl.loop(0, tiles // 2)(expand)
+    acc[...] = jnp.zeros(acc.shape, jnp.float32)
+    load_basis.wait()
+    cuts = [tiles * d // line for d in range(line + 1)]
+    pl.loop(cuts[0], cuts[1])(expand)
 
     passed = []
     for d in range(1, line):
@@ -139,19 +160,7 @@
         )
         copy.start()
         passed.append(copy)
-
-    pl.loop(tiles // 2, tiles)(expand)
-
-    for d in range(1, col_count):
-        origin = col_at(d)
-        remote(
-            packed, by_col.at[origin], col_send.at[d], col_recv.at[origin], row, origin
-        ).wait_recv()
-    for d in range(line):
-        origin = 2 * lax.rem(place + line - d, line) + 1 - side
-        remote(
-            packed, by_row.at[origin], row_send.at[0], row_recv.at[origin], partner, col
-        ).wait_recv()
+        pl.loop(cuts[d], cuts[d + 1])(expand)
 
     def widen_row(r):
         for l in range(row_blocks):
@@ -162,7 +171,52 @@
                 dh, dl, at, 0, pairs,
             )
 
-    pl.loop(0, row_count)(widen_row)
+    step = 4 * G
+
+    def absorb(r):
+        widen_row(r)
+        deep = pl.ds(pl.multiple_of(r * rows, PAIR), rows)
+
+        @pl.loop(0, points // step)
+        def _(s):
+            at = pl.ds(pl.multiple_of(s * step, step), step)
+            acc[at, :] += dot3(bh[at, deep], bl[at, deep], dh[deep, :], dl[deep, :])
+
+    @pl.loop(0, line)
+    def _(d):
+        absorb(on_line(d))
+
+    @pl.loop(0, line)
+    def _(d):
+        origin = 2 * lax.rem(place + line - d, line) + 1 - side
+        remote(
+            packed, by_row.at[origin], row_send.at[0], row_recv.at[origin], partner, col
+        ).wait_recv()
+        absorb(origin)
+
+    mine = pl.ds(pl.multiple_of(col * width, PAIR), width)
+
+    @pl.loop(0, tiles)
+    def _(t):
+        at = pl.ds(pl.multiple_of(t * G, G), G)
+        local = bh[at, mine].astype(jnp.float32) + bl[at, mine].astype(jnp.float32)
+        sums = jnp.sum(acc[at, :] * local, axis=1, keepdims=True)
+        parts_out[pl.ds(t, 1), :] = jnp.broadcast_to(sums, (G, G)).T[0:1, :]
+
+    part_sends = []
+    for d in range(1, col_count):
+        copy = remote(
+            parts_out, parts_in.at[col], part_send.at[d], part_recv.at[col], row, col_at(d)
+        )
+        copy.start()
+        part_sends.append(copy)
+    parts_in[col] = parts_out[...]
+
+    for d in range(1, col_count):
+        origin = col_at(d)
+        remote(
+            packed, by_col.at[origin], col_send.at[d], col_recv.at[origin], row, origin
+        ).wait_recv()
     for c in range(col_count):
         for l in range(row_blocks):
             widen(
@@ -170,20 +224,6 @@
                 by_col[c, rows + l : rows + l + 1, :],
                 oh, ol, l * BS, c * width, pairs,
             )
-
-    step = 4 * G
-    mine = pl.ds(pl.multiple_of(col * width, PAIR), width)
-
-    @pl.loop(0, points // step)
-    def _(s):
-        at = pl.ds(pl.multiple_of(s * step, step), step)
-        x = dot3(bh[at, :], bl[at, :], dh[...], dl[...])
-        local = bh[at, mine].astype(jnp.float32) + bl[at, mine].astype(jnp.float32)
-        sums = jnp.sum(x * local, axis=1, keepdims=True)
-        for t in range(step // G):
-            tile = jnp.broadcast_to(sums[t * G : (t + 1) * G], (G, G))
-            parts_out[pl.ds(s * (step // G) + t, 1), :] = tile.T[0:1, :]
-
     product[...] = dot3(oh[...], ol[...], dh[...], dl[...])
     total = jnp.zeros((BS, PAIR), jnp.float32)
     for l in range(row_blocks):
@@ -198,16 +238,14 @@
         kept[l * BS : (l + 1) * BS, :] = block
         total += block * block
     square = jnp.sum(jnp.sum(total, axis=1, keepdims=True), axis=0, keepdims=True)
-    parts_out[tiles : tiles + 8, :] = jnp.broadcast_to(square, (8, PAIR))
-
-    part_sends = []
+    square_out[...] = jnp.broadcast_to(square, (8, PAIR))
     for d in range(1, col_count):
         copy = remote(
-            parts_out, parts_in.at[col], part_send.at[d], part_recv.at[col], row, col_at(d)
+            square_out, square_in.at[col], square_send.at[d], square_recv.at[col], row, col_at(d)
         )
         copy.start()
         part_sends.append(copy)
-    parts_in[col] = parts_out[...]
+    square_in[col] = square_out[...]
     for t in range(tiles):
         at = pl.ds(t * G, G)
         local = bh[at, mine].astype(jnp.float32) + bl[at, mine].astype(jnp.float32)
@@ -220,14 +258,22 @@
     sums = parts_in[0]
     for c in range(1, col_count):
         sums += parts_in[c]
-    potential = weights[...] * jnp.tanh(sums[0:tiles, :])
+    potential = weights[...] * jnp.tanh(sums)
     for t in range(tiles):
         high, low = split(turned[:, t * G : (t + 1) * G] * potential[t : t + 1, :])
         wh[:, t * G : (t + 1) * G] = high
         wl[:, t * G : (t + 1) * G] = low
     lanes = core.shape[0]
     stored = ks_slots * BS
-    square_all = jnp.broadcast_to(sums[tiles : tiles + 1, 0:1], (8, lanes))
+    for d in range(1, col_count):
+        origin = col_at(d)
+        remote(
+            square_out, square_in.at[origin], square_send.at[d], square_recv.at[origin], row, origin
+        ).wait_recv()
+    squares = square_in[0]
+    for c in range(1, col_count):
+        squares += square_in[c]
+    square_all = jnp.broadcast_to(squares[0:1, 0:1], (8, lanes))
 
     def contribute(owner, out, i):
         at = pl.ds(pl.multiple_of(owner * lanes, PAIR), lanes)
@@ -354,16 +400,11 @@
     rows = row_blocks * BS
     line = row_count // 2
     stored = ks_slots * BS
-    col = lax.axis_index("col")
     f32, bf16 = jnp.float32, jnp.bfloat16
     vmem, smem = pl.BlockSpec(memory_space=pltpu.VMEM), pl.BlockSpec(memory_space=pltpu.SMEM)
 
-    local_codes = jnp.repeat((density_cols - col * col_blocks).astype(f32), BS, axis=1)
-    local_ks = jnp.repeat((ks_cols - col * col_blocks).astype(f32).T, BS, axis=1)
-    ks_lines = [local_ks[:, at : at + PAIR] for at in range(0, rows, PAIR)]
     used = rows + row_blocks + ks_slots * (rows // PAIR)
-    fill = jnp.zeros((-used % 16, PAIR), f32)
-    packed = jnp.concatenate([density_values, local_codes, *ks_lines, fill], axis=0)
+    packed_rows = used + -used % 16
 
     blocks = jnp.arange(all_blocks, dtype=jnp.int32)
     index = jnp.arange(TB, dtype=jnp.int32)
@@ -377,7 +418,6 @@
         ks_slots=ks_slots,
         entry_count=float(order * own_slots * col_count * BS),
     )
-    packed_rows = packed.shape[0]
     return tuple(
         pl.pallas_call(
             kernel,
@@ -385,9 +425,14 @@
                 jax.ShapeDtypeStruct((rows, stored), f32),
                 jax.ShapeDtypeStruct((rows, PAIR), f32),
             ],
-            in_specs=[smem] + [vmem] * 4,
+            in_specs=[smem] * 3 + [pl.BlockSpec(memory_space=pl.ANY)] + [vmem] * 3,
             out_specs=[vmem, vmem],
             scratch_shapes=[
+                pltpu.VMEM(basis_values.shape, f32),
+                pltpu.VMEM((packed_rows, PAIR), f32),
+                pltpu.VMEM((points, width), f32),
+                pltpu.VMEM((8, PAIR), f32),
+                pltpu.VMEM((col_count, 8, PAIR), f32),
                 pltpu.VMEM((points, order), bf16),
                 pltpu.VMEM((points, order), bf16),
                 pltpu.VMEM((2, TB // 2 + 1, G, PAIR), f32),
@@ -399,8 +444,8 @@
                 pltpu.VMEM((rows, order), bf16),
                 pltpu.VMEM((rows, width), f32),
                 pltpu.VMEM((rows, PAIR), f32),
-                pltpu.VMEM((tiles + 8, PAIR), f32),
-                pltpu.VMEM((col_count, tiles + 8, PAIR), f32),
+                pltpu.VMEM((tiles, PAIR), f32),
+                pltpu.VMEM((col_count, tiles, PAIR), f32),
                 pltpu.VMEM((width, points), f32),
                 pltpu.VMEM((width, points), bf16),
                 pltpu.VMEM((width, points), bf16),
@@ -420,6 +465,9 @@
                 dma((line,)),
                 dma((line,)),
                 dma((line,)),
+                dma((col_count,)),
+                dma((col_count,)),
+                dma,
             ],
             compiler_params=pltpu.CompilerParams(
                 vmem_limit_bytes=VMEM_BUDGET, collective_id=0, has_side_effects=True
@@ -430,7 +478,9 @@
                 transcendentals=points,
             ),
             name="kohn_sham_build",
-        )(places, basis_values, packed, grid_weights, core_hamiltonian)
+        )(
+            places, density_cols, ks_cols, basis_values, density_values, grid_weights, core_hamiltonian
+        )
     )
 
 
@@ -441,7 +491,7 @@
     width = order // lax.axis_size("col")
     points = tile_blocks.shape[0] * G
     held = 4 * points * order + 4 * order * width + 4 * points * TB * BS
-    fits = held + 16 * points * width < VMEM_BUDGET
+    fits = held + 24 * points * width < VMEM_BUDGET
     regular = density_cols.shape[1] * BS == PAIR and density_cols.shape[0] % 2 == 0
     regular = regular and lax.axis_size("row") % 2 == 0
     if fits and regular and width % PAIR == 0 and tile_blocks.shape[0] % 8 == 0:

time: 83.9 us -> 80 us (0.954)
  Pallas kernels: 76.3 us -> 73 us
  other arithmetic: 2.15 us -> 0.78 us
  local copies, waits for them, and re-layouts: 4.46 us -> 5.34 us
    pallas_call x1, Pallas kernels: 76.3 us -> 73 us  [dense(): pl.pallas_call(kernel, out_shape=[jax.ShapeDtypeStruct((rows, stored), f3...]
    unnamed x6 -> x11, local copies, waits for them, and re-layouts: 3 us -> 5.34 us
    concatenate x1 -> x0, local copies, waits for them, and re-layouts: 0.96 us -> none  [dense(): jnp.concatenate([density_values, local_codes, *ks_lines, fill], axis=0)]
where the time goes in v1:
time: 80 us; the launch traced here: 79.7 us
  Pallas kernels  73 us (91%)
  local copies, waits for them, and re-layouts  5.34 us (7%)
    pallas_call x1, Pallas kernels, dense(): pl.pallas_call(kernel, out_shape=[jax.ShapeDtypeStruct((rows, stored), f3...  73 us
    unnamed x11, local copies, waits for them, and re-layouts  5.34 us

profile of v1, /device:TPU:9, one launch (start us, length us, event | category | flops | bytes accessed | tf_op | source)
XLA Modules:
  0.0 79.7 jit_solution(9386965657134349732)
XLA Ops:
  0.6 0.8 copy.10.density_cols
  1.4 0.8 select_reduce_fusion.places
  2.2 0.0 copy-start
  2.2 0.9 %copy-done = f32[256,256]{1,0:T(8,128)S(1)} copy-done((f32[256,256]{1,0:T(8,128)S(1)}, f32[256,256]{1,0:T(8,128)}, u32[]{:S(2)}) %copy-start) | copy-done | bytes 262168
  3.1 0.0 copy-start.1
  3.1 0.9 %copy-done.1 = f32[256,128]{1,0:T(8,128)S(1)} copy-done((f32[256,128]{1,0:T(8,128)S(1)}, f32[256,128]{1,0:T(8,128)}, u32[]{:S(2)}) %copy-start.1) | copy-done | bytes 131096
  4.0 0.0 copy-start.2
  4.0 0.7 copy-done.2
  4.7 0.0 copy-start.3
  4.7 0.7 copy-done.3
  5.4 73.0 %kohn_sham_build.1 = (f32[256,256]{1,0:T(8,128)S(1)}, f32[256,128]{1,0:T(8,128)S(1)}) custom-call(s32[8,32]{1,0:T(8,128)S(1)} %select_reduce_fusion.places, s32[4,2]{1,0:T(4,128)S(1)} %copy.10.density_cols, s32[4,4]{1,0:T(4,128)S(1)} %copy-done.3, f32[8,128,1024]{2,1,0:T(8,128)} %basis_hbm.1, f32[256,128]{1,0:T(8,128)S(1)} %copy-done.1, ...), custom_call_target="tpu_custom_call" | custom-call | flops 12884901888 | bytes 4194304 | tf_op jit(solution)/shard_map/kohn_sham_build/pallas_call | solution.py:422
  78.4 0.7 copy.13
  79.1 0.7 copy.14
Async XLA Ops:
  2.2 1.0 %copy-start = (f32[256,256]{1,0:T(8,128)S(1)}, f32[256,256]{1,0:T(8,128)}, u32[]{:S(2)}) copy-start(f32[256,256]{1,0:T(8,128)} %core.1) | copy-start | bytes 786436
  3.1 0.9 %copy-start.1 = (f32[256,128]{1,0:T(8,128)S(1)}, f32[256,128]{1,0:T(8,128)}, u32[]{:S(2)}) copy-start(f32[256,128]{1,0:T(8,128)} %values.1) | copy-start | bytes 393220
  4.0 0.7 copy-start.2
  4.7 0.7 copy-start.3

commit v2 on v1

--- a/solution.py
+++ b/solution.py
@@ -146,8 +146,28 @@
 
     acc[...] = jnp.zeros(acc.shape, jnp.float32)
     load_basis.wait()
-    cuts = [tiles * d // line for d in range(line + 1)]
-    pl.loop(cuts[0], cuts[1])(expand)
+    first = tiles // 2 if line > 1 else tiles
+    pl.loop(0, first)(expand)
+
+    def widen_row(r):
+        for l in range(row_blocks):
+            at = pl.multiple_of((r * row_blocks + l) * BS, BS)
+            widen(
+                by_row[r, l * BS : (l + 1) * BS, :],
+                by_row[r, rows + l : rows + l + 1, :],
+                dh, dl, at, 0, pairs,
+            )
+
+    step = 4 * G
+
+    def absorb(r):
+        widen_row(r)
+        deep = pl.ds(pl.multiple_of(r * rows, PAIR), rows)
+
+        @pl.loop(0, points // step)
+        def _(s):
+            at = pl.ds(pl.multiple_of(s * step, step), step)
+            acc[at, :] += dot3(bh[at, deep], bl[at, deep], dh[deep, :], dl[deep, :])
 
     passed = []
     for d in range(1, line):
@@ -160,31 +180,14 @@
         )
         copy.start()
         passed.append(copy)
-        pl.loop(cuts[d], cuts[d + 1])(expand)
-
-    def widen_row(r):
-        for l in range(row_blocks):
-            at = pl.multiple_of((r * row_blocks + l) * BS, BS)
-            widen(
-                by_row[r, l * BS : (l + 1) * BS, :],
-                by_row[r, rows + l : rows + l + 1, :],
-                dh, dl, at, 0, pairs,
-            )
-
-    step = 4 * G
-
-    def absorb(r):
-        widen_row(r)
-        deep = pl.ds(pl.multiple_of(r * rows, PAIR), rows)
-
-        @pl.loop(0, points // step)
-        def _(s):
-            at = pl.ds(pl.multiple_of(s * step, step), step)
-            acc[at, :] += dot3(bh[at, deep], bl[at, deep], dh[deep, :], dl[deep, :])
-
-    @pl.loop(0, line)
+        if d == 1:
+            pl.loop(first, tiles)(expand)
+        else:
+            absorb(2 * lax.rem(place + line - d + 2, line) + side)
+
+    @pl.loop(max(line - 2, 0), line)
     def _(d):
-        absorb(on_line(d))
+        absorb(2 * lax.rem(place + line - d, line) + side)
 
     @pl.loop(0, line)
     def _(d):

time: 80 us -> 78 us (0.975)
  Pallas kernels: 73 us -> 70.9 us
    pallas_call x1, Pallas kernels: 73 us -> 70.9 us  [dense(): pl.pallas_call(kernel, out_shape=[jax.ShapeDtypeStruct((rows, stored), f3...]
where the time goes in v2:
time: 78 us; the launch traced here: 77.7 us
  Pallas kernels  70.9 us (91%)
  local copies, waits for them, and re-layouts  5.34 us (7%)
  other arithmetic  0.78 us (1%)
    pallas_call x1, Pallas kernels, dense(): pl.pallas_call(kernel, out_shape=[jax.ShapeDtypeStruct((rows, stored), f3...  70.9 us
    unnamed x11, local copies, waits for them, and re-layouts  5.34 us

profile of v2, /device:TPU:9, one launch (start us, length us, event | category | flops | bytes accessed | tf_op | source)
XLA Modules:
  0.0 77.7 jit_solution(6708721694973233077)
XLA Ops:
  0.6 0.8 copy.10.density_cols
  1.4 0.8 %select_reduce_fusion.places = s32[8,32]{1,0:T(8,128)S(1)} fusion(s32[8,16]{1,0:T(8,128)} %param.11), kind=kLoop, calls=%fused_computation | loop fusion | flops 12032 | bytes 1536 | tf_op jit(solution)/shard_map/reduce_min | solution.py:415
  2.2 0.0 copy-start
  2.2 0.9 %copy-done = f32[256,256]{1,0:T(8,128)S(1)} copy-done((f32[256,256]{1,0:T(8,128)S(1)}, f32[256,256]{1,0:T(8,128)}, u32[]{:S(2)}) %copy-start) | copy-done | bytes 262168
  3.1 0.0 copy-start.1
  3.1 0.9 %copy-done.1 = f32[256,128]{1,0:T(8,128)S(1)} copy-done((f32[256,128]{1,0:T(8,128)S(1)}, f32[256,128]{1,0:T(8,128)}, u32[]{:S(2)}) %copy-start.1) | copy-done | bytes 131096
  4.0 0.0 copy-start.2
  4.0 0.7 copy-done.2
  4.7 0.0 copy-start.3
  4.7 0.7 copy-done.3
  5.4 70.9 %kohn_sham_build.1 = (f32[256,256]{1,0:T(8,128)S(1)}, f32[256,128]{1,0:T(8,128)S(1)}) custom-call(s32[8,32]{1,0:T(8,128)S(1)} %select_reduce_fusion.places, s32[4,2]{1,0:T(4,128)S(1)} %copy.10.density_cols, s32[4,4]{1,0:T(4,128)S(1)} %copy-done.3, f32[8,128,1024]{2,1,0:T(8,128)} %basis_hbm.1, f32[256,128]{1,0:T(8,128)S(1)} %copy-done.1, ...), custom_call_target="tpu_custom_call" | custom-call | flops 12884901888 | bytes 4194304 | tf_op jit(solution)/shard_map/kohn_sham_build/pallas_call | solution.py:425
  76.3 0.7 copy.13
  77.0 0.7 copy.14
Async XLA Ops:
  2.2 1.0 %copy-start = (f32[256,256]{1,0:T(8,128)S(1)}, f32[256,256]{1,0:T(8,128)}, u32[]{:S(2)}) copy-start(f32[256,256]{1,0:T(8,128)} %core.1) | copy-start | bytes 786436
  3.1 0.9 %copy-start.1 = (f32[256,128]{1,0:T(8,128)S(1)}, f32[256,128]{1,0:T(8,128)}, u32[]{:S(2)}) copy-start(f32[256,128]{1,0:T(8,128)} %values.1) | copy-start | bytes 393220
  4.0 0.7 copy-start.2
  4.7 0.7 copy-start.3
